TPU v7x, 32 devices: a whole 2x2x4 slice. The times are simulated.
32 devices in a mesh: seg: 8 (over z, x), sub: 4 (over y, core).
Axes of the slice: x: 2, y: 2, z: 4, core: 2. Of those that a mesh axis runs over, the one named last changes fastest.
Arguments:
- start_state: float32 [2, 27, 16384], P(None, None, ('seg', 'sub')), may hold values from -6 to 6
- right_side: float32 [2, 27, 16384], P(None, None, ('seg', 'sub')), may hold values from -3 to 3
- previous: float32 [27, 16384], P(None, ('seg', 'sub')), may hold values from -0.9 to 0.9
- refined: int32 [16384], P(('seg', 'sub')), may hold values 0 or 1
- old_cuts: int32 [8, 5], P('seg'), may hold values from 0 to 1024, as said below
- new_cuts: int32 [8, 5], P('seg'), may hold values from 0 to 1024, as said below
- face_links: int32 [6, 16384], P(None, ('seg', 'sub')), may hold values from -1 to 639
Outputs:
- smoothed: float32 [2, 27, 16384], P(None, None, ('seg', 'sub'))
Inputs may be any that keep to these rules, and one draw needn't show every extreme that they name: `old_cuts`: each row begins with 0 and ends with 1024; consecutive cuts differ by 128 to 384, and in every row some difference is exactly 384. `new_cuts`: each row begins with 0 and ends with 1024 and never falls; every other cut lies within 64 positions of the old cut of the same index; in every row one cut lies exactly 64 before its old cut and the next one exactly 64 after, so that some device's new count is 512; no new count exceeds 512. `face_links`: entry (face, e) names the element across that face of new slot e: a value below 512 is a slot of the same device, 512 + g is slot g of device (s-1, u), 576 + g slot g of device (s+1, u), -1 the domain's boundary; faces in the order -x, +x, -y, +y, -z, +z. 1 marks a refined element.
All inputs are finite; a program needn't handle non-finite values. No bound on the sum of `refined` on one device may be relied on, other than what follows from the above.
Results may differ from a plain program's by a relative error of at most 0.0001.
Values sent between devices are 32-bit elements; how exact they have to be, the bound alone decides.
A program may use at most 64 MiB of HBM per device.

v0:
```python
import jax
import jax.numpy as jnp
import numpy as np
from jax import lax
from jax.sharding import PartitionSpec as P

SWEEPS = 3


time_step = 0.01
gradient_energy = 0.01
penalty = 2.0


def from_behind(block, axis, distance):
    devices = range(lax.axis_size(axis))
    route = [(i - distance, i) for i in devices if i - distance in devices]
    return lax.ppermute(block, axis, route)


def extended_2(cells, sides, width):
    for axis, dim in sides:
        count = lax.axis_size(axis)
        ends = count - 1
        head = lax.slice_in_dim(cells, 0, width, axis=dim)
        tail = lax.slice_in_dim(cells, cells.shape[dim] - width, cells.shape[dim], axis=dim)
        cells = jnp.concatenate(
            [
                lax.ppermute(tail, axis, [(i, (i + 1) % count) for i in range(ends)]),
                cells,
                lax.ppermute(head, axis, [((i + 1) % count, i) for i in range(ends)]),
            ],
            axis=dim,
        )
    return cells


def element_tables():
    weights = np.array([0.5, 2.0, 0.5])
    slope_table = np.array([[7.0, -8.0, 1.0], [-8.0, 16.0, -8.0], [1.0, -8.0, 7.0]]) / 6.0
    diagonal = np.array([[0.5, 0.0, 0.0], [0.0, 2.0, 0.0], [0.0, 0.0, 0.5]])
    stiffness = (
        np.kron(slope_table, np.kron(diagonal, diagonal))
        + np.kron(diagonal, np.kron(slope_table, diagonal))
        + np.kron(diagonal, np.kron(diagonal, slope_table))
    )
    mass_table = np.kron(weights, np.kron(weights, weights))
    across = np.zeros((6, 9), np.int32)
    face_map = np.zeros((27, 54))
    face_diag = np.zeros(27)
    for direction in range(3):
        for side_index in range(2):
            surface = 2 * direction + side_index
            for major_index in range(3):
                for minor_index in range(3):
                    inner_index = major_index * 3 + minor_index
                    near_side = [major_index, minor_index]
                    near_side.insert(direction, 2 * side_index)
                    far_side = [major_index, minor_index]
                    far_side.insert(direction, 2 - 2 * side_index)
                    near_node = near_side[0] * 9 + near_side[1] * 3 + near_side[2]
                    far_node = far_side[0] * 9 + far_side[1] * 3 + far_side[2]
                    across[surface, inner_index] = far_node
                    face_weight = weights[major_index] * weights[minor_index]
                    face_map[near_node, surface * 9 + inner_index] = face_weight
                    face_diag[near_node] += face_weight
    return (
        jnp.asarray(stiffness, jnp.float32),
        jnp.asarray(mass_table, jnp.float32),
        jnp.asarray(face_diag, jnp.float32),
        jnp.asarray(face_map, jnp.float32),
        across,
    )


def exchange_heads(iterate, ghost_width):
    leading = iterate[:, :, :ghost_width].reshape(54, ghost_width)
    below_rows = from_behind(leading, "seg", 1)
    above_rows = from_behind(leading, "seg", -1)
    return (below_rows, above_rows)


def laplace_part(iterate, face_links, tables, stiff_scale, ghost_width):
    stiffness, mass_table, face_diag, face_map, across = tables
    below_rows, above_rows = exchange_heads(iterate, ghost_width)
    capacity = iterate.shape[-1]
    extended = jnp.concatenate([iterate.reshape(54, capacity), below_rows, above_rows], 1)
    extended = extended.reshape(2, 27, capacity + 2 * ghost_width)
    pieces = []
    for surface in range(6):
        face_rows = extended[:, across[surface]]
        targets = face_links[surface]
        clamped = jnp.where(targets >= 0, targets, 0)
        picked = jnp.take(face_rows, clamped, axis=2)
        pieces.append(picked * (targets >= 0).astype(jnp.float32)[None, None, :])
    gathered = jnp.concatenate(pieces, 1)
    local_part = jnp.einsum("mn,fnc->fmc", stiffness, iterate, precision=lax.Precision.HIGHEST)
    coupled = jnp.einsum("mk,fkc->fmc", face_map, gathered, precision=lax.Precision.HIGHEST)
    return stiff_scale[None, None, :] * (
        local_part + penalty * (face_diag[:, None] * iterate - coupled)
    )


def local(start_state, right_side, previous, refined, old_cuts, new_cuts, face_links):
    tables = element_tables()
    capacity = start_state.shape[-1]
    quarter = capacity // 8
    ghost_width = capacity // 8
    sub_index = lax.axis_index("sub")
    old_first = old_cuts[0, sub_index]
    old_end = old_cuts[0, sub_index + 1]
    new_first = new_cuts[0, sub_index]
    new_end = new_cuts[0, sub_index + 1]
    packed = jnp.concatenate(
        [
            start_state.reshape(54, capacity),
            right_side.reshape(54, capacity),
            previous,
            refined.astype(jnp.float32)[None, :],
        ],
        0,
    )
    head_rows = packed[:, :quarter]
    tail_rows = lax.dynamic_slice_in_dim(packed, old_end - old_first - quarter, quarter, 1)
    rim_rows = extended_2(jnp.concatenate([head_rows, tail_rows], 1), (("sub", 1),), quarter)
    extended = jnp.concatenate([rim_rows[:, :quarter], packed, rim_rows[:, 3 * quarter :]], 1)
    slot_index = jnp.arange(capacity, dtype=jnp.int32)
    position = new_first + slot_index
    source_index = jnp.where(
        position < old_end, position - old_first + quarter, quarter + capacity + position - old_end
    )
    occupied = slot_index < new_end - new_first
    source_index = jnp.where(occupied, source_index, 0)
    moved = jnp.take(extended, source_index, axis=1) * occupied.astype(jnp.float32)[None, :]
    iterate = moved[:54].reshape(2, 27, capacity)
    target = moved[54:108].reshape(2, 27, capacity)
    prior = moved[108:135]
    flag_row = moved[135]
    mass_scale = 1.0 - 0.875 * flag_row
    stiff_scale = 1.0 - 0.5 * flag_row
    mobility = 1.0 - prior * prior
    curvature = 3.0 * prior * prior - 1.0
    lumped = tables[1][:, None] * mass_scale[None, :]
    center = 1.0
    half_width = 0.5
    spread_ratio = center / half_width
    weight_prev = 1.0 / spread_ratio
    update = jnp.zeros_like(iterate)
    for sweep_index in range(SWEEPS):
        laplace = laplace_part(iterate, face_links, tables, stiff_scale, ghost_width)
        concentration = lumped * iterate[0] + time_step * mobility * laplace[1]
        potential = (
            lumped * iterate[1] - curvature * (lumped * iterate[0]) - gradient_energy * laplace[0]
        )
        residual = target - jnp.stack([concentration, potential], 0)
        scaled = residual / lumped[None]
        if sweep_index == 0:
            update = scaled / center
        else:
            weight_now = 1.0 / (2.0 * spread_ratio - weight_prev)
            update = weight_now * weight_prev * update + 2.0 * weight_now / half_width * scaled
            weight_prev = weight_now
        iterate = iterate + update
    return iterate


def solution(mesh):
    placed = (
        P(None, None, ("seg", "sub")),
        P(None, None, ("seg", "sub")),
        P(None, ("seg", "sub")),
        P(("seg", "sub")),
        P("seg", None),
        P("seg", None),
        P(None, ("seg", "sub")),
    )
    return jax.shard_map(
        local, mesh=mesh, in_specs=placed, out_specs=P(None, None, ("seg", "sub")), check_vma=False
    )
```

profile of v0, /device:TPU:20, one launch (start us, length us, event | category | flops | bytes accessed | tf_op | source)
XLA Modules:
  0.0 116.2 jit_solution(6075797614499771315)
XLA Ops:
  6.9 1.9 %collective-permute-start = (f32[136,64]{0,1:T(8,128)S(1)}, f32[136,64]{0,1:T(8,128)S(1)}, u32[]{:S(2)}, u32[]{:S(2)}) collective-permute-start(f32[136,64]{0,1:T(8,128)S(1)} %get-tuple-element.10), channel_id=1, source_target_pairs={{0,1},{1,2},{2,3},{4,5},{5,6},{6,7},{8,9},{9,10},{10,11},{12,13},{... | collective-permute-start | bytes 104456 | tf_op jit(solution)/shard_map/ppermute | solution.py:29
  8.9 3.6 %collective-permute-start.1 = (f32[136,64]{0,1:T(8,128)S(1)}, f32[136,64]{0,1:T(8,128)S(1)}, u32[]{:S(2)}, u32[]{:S(2)}) collective-permute-start(f32[136,64]{0,1:T(8,128)S(1)} %get-tuple-element.11), channel_id=1, source_target_pairs={{1,0},{2,1},{3,2},{5,4},{6,5},{7,6},{9,8},{10,9},{11,10},{13,12},{... | collective-permute-start | bytes 104456 | tf_op jit(solution)/shard_map/ppermute | solution.py:31
  13.8 2.0 %compare_select_fusion = s32[512,1]{0,1:T(1,128)S(1)} fusion(s32[]{:T(128)} %bitcast.3, s32[]{:T(128)} %bitcast.2, s32[]{:T(128)} %bitcast.1, s32[]{:T(128)S(6)} %sub.106), kind=kLoop, calls=%fused_computation.133 | loop fusion | flops 6144 | bytes 2064 | tf_op jit(solution)/shard_map/jit(_take)/jit(_where)/select_n | solution.py:134
  18.7 2.0 %compare_and_fusion.6 = pred[512]{0:T(512)(128)(4,1)S(1)} fusion(s32[]{:T(128)} %bitcast.3, s32[]{:T(128)} %bitcast.2, s32[]{:T(128)} %bitcast.1, s32[]{:T(128)S(6)} %sub.106), kind=kLoop, calls=%fused_computation.180 | loop fusion | flops 7680 | bytes 528 | tf_op jit(solution)/shard_map/jit(_take)/and | solution.py:134
  21.1 1.6 %gather_fusion = f32[512,136]{1,0:T(8,128)S(1)} fusion(f32[136,640]{0,1:T(8,128)S(1)} %pad_maximum_fusion, s32[1024]{0:T(1024)S(1)} %pad_clamp_fusion.12), kind=kCustom, calls=%fused_computation.18 | custom fusion | bytes 559104 | tf_op jit(solution)/shard_map/jit(_take)/gather | solution.py:134
  23.0 3.3 %collective-permute-start.3 = (f32[54,64]{1,0:T(8,128)S(1)}, f32[54,64]{1,0:T(8,128)S(1)}, u32[]{:S(2)}, u32[]{:S(2)}) collective-permute-start(f32[54,64]{1,0:T(8,128)S(1)} %reshape.186), channel_id=1, source_target_pairs={{4,0},{8,4},{12,8},{16,12},{20,16},{24,20},{28,24},{5,1},{9,5},{13... | collective-permute-start | bytes 41480 | tf_op jit(solution)/shard_map/ppermute | solution.py:18
  26.3 2.6 %collective-permute-start.2 = (f32[54,64]{1,0:T(8,128)S(1)}, f32[54,64]{1,0:T(8,128)S(1)}, u32[]{:S(2)}, u32[]{:S(2)}) collective-permute-start(f32[54,64]{1,0:T(8,128)S(1)} %reshape.186), channel_id=1, source_target_pairs={{0,4},{4,8},{8,12},{12,16},{16,20},{20,24},{24,28},{1,5},{5,9},{9,... | collective-permute-start | bytes 41480 | tf_op jit(solution)/shard_map/ppermute | solution.py:18
  28.8 4.1 %collective-permute-done.2 = f32[54,64]{1,0:T(8,128)S(1)} collective-permute-done((f32[54,64]{1,0:T(8,128)S(1)}, f32[54,64]{1,0:T(8,128)S(1)}, u32[]{:S(2)}, u32[]{:S(2)}) %collective-permute-start.2) | collective-permute-done | bytes 13856 | tf_op jit(solution)/shard_map/ppermute | solution.py:18
  37.1 2.1 %gather_fusion.20 = f32[512,2,9]{2,1,0:T(2,128)S(1)} fusion(f32[2,9,640]{1,0,2:T(2,128)S(1)} %copy.64, s32[1024]{0:T(1024)S(1)} %pad_clamp_fusion.8), kind=kCustom, calls=%fused_computation.1.clone | custom fusion | bytes 75776 | tf_op jit(solution)/shard_map/jit(_take)/gather | solution.py:94
  39.7 2.1 %gather_fusion.19 = f32[512,2,9]{2,1,0:T(2,128)S(1)} fusion(f32[2,9,640]{1,0,2:T(2,128)S(1)} %copy.61, s32[1024]{0:T(1024)S(1)} %pad_clamp_fusion.10), kind=kCustom, calls=%fused_computation.clone | custom fusion | bytes 75776 | tf_op jit(solution)/shard_map/jit(_take)/gather | solution.py:94
  42.3 2.1 %gather_fusion.21 = f32[512,2,9]{2,1,0:T(2,128)S(1)} fusion(f32[2,9,640]{1,0,2:T(2,128)S(1)} %copy.67, s32[1024]{0:T(1024)S(1)} %pad_clamp_fusion.6), kind=kCustom, calls=%fused_computation.2.clone | custom fusion | bytes 75776 | tf_op jit(solution)/shard_map/jit(_take)/gather | solution.py:94
  44.9 2.1 %gather_fusion.22 = f32[512,2,9]{2,1,0:T(2,128)S(1)} fusion(f32[2,9,640]{1,0,2:T(2,128)S(1)} %copy.70, s32[1024]{0:T(1024)S(1)} %pad_clamp_fusion.4), kind=kCustom, calls=%fused_computation.3.clone | custom fusion | bytes 75776 | tf_op jit(solution)/shard_map/jit(_take)/gather | solution.py:94
  47.5 2.1 %gather_fusion.23 = f32[512,2,9]{2,1,0:T(2,128)S(1)} fusion(f32[2,9,640]{1,0,2:T(2,128)S(1)} %copy.73, s32[1024]{0:T(1024)S(1)} %pad_clamp_fusion.2), kind=kCustom, calls=%fused_computation.4.clone | custom fusion | bytes 75776 | tf_op jit(solution)/shard_map/jit(_take)/gather | solution.py:94
  50.1 2.1 %gather_fusion.24 = f32[512,2,9]{2,1,0:T(2,128)S(1)} fusion(f32[2,9,640]{1,0,2:T(2,128)S(1)} %copy.76, s32[1024]{0:T(1024)S(1)} %pad_clamp_fusion), kind=kCustom, calls=%fused_computation.5.clone | custom fusion | bytes 75776 | tf_op jit(solution)/shard_map/jit(_take)/gather | solution.py:94
  55.2 1.9 %collective-permute-start.5 = (f32[54,64]{1,0:T(8,128)S(1)}, f32[54,64]{1,0:T(8,128)S(1)}, u32[]{:S(2)}, u32[]{:S(2)}) collective-permute-start(f32[54,64]{1,0:T(8,128)S(1)} %reshape.188), channel_id=1, source_target_pairs={{4,0},{8,4},{12,8},{16,12},{20,16},{24,20},{28,24},{5,1},{9,5},{13... | collective-permute-start | bytes 41480 | tf_op jit(solution)/shard_map/ppermute | solution.py:18
  57.2 4.1 %collective-permute-start.4 = (f32[54,64]{1,0:T(8,128)S(1)}, f32[54,64]{1,0:T(8,128)S(1)}, u32[]{:S(2)}, u32[]{:S(2)}) collective-permute-start(f32[54,64]{1,0:T(8,128)S(1)} %reshape.188), channel_id=1, source_target_pairs={{0,4},{4,8},{8,12},{12,16},{16,20},{20,24},{24,28},{1,5},{5,9},{9,... | collective-permute-start | bytes 41480 | tf_op jit(solution)/shard_map/ppermute | solution.py:18
  61.5 2.4 %collective-permute-done.4 = f32[54,64]{1,0:T(8,128)S(1)} collective-permute-done((f32[54,64]{1,0:T(8,128)S(1)}, f32[54,64]{1,0:T(8,128)S(1)}, u32[]{:S(2)}, u32[]{:S(2)}) %collective-permute-start.4) | collective-permute-done | bytes 13856 | tf_op jit(solution)/shard_map/ppermute | solution.py:18
  67.9 2.1 %gather_fusion.26 = f32[512,2,9]{2,1,0:T(2,128)S(1)} fusion(f32[2,9,640]{1,0,2:T(2,128)S(1)} %copy.83, s32[1024]{0:T(1024)S(1)} %pad_clamp_fusion.8), kind=kCustom, calls=%fused_computation.7.clone | custom fusion | bytes 75776 | tf_op jit(solution)/shard_map/jit(_take)/gather | solution.py:94
  70.6 2.1 %gather_fusion.25 = f32[512,2,9]{2,1,0:T(2,128)S(1)} fusion(f32[2,9,640]{1,0,2:T(2,128)S(1)} %copy.81, s32[1024]{0:T(1024)S(1)} %pad_clamp_fusion.10), kind=kCustom, calls=%fused_computation.6.clone | custom fusion | bytes 75776 | tf_op jit(solution)/shard_map/jit(_take)/gather | solution.py:94
  73.2 2.1 %gather_fusion.27 = f32[512,2,9]{2,1,0:T(2,128)S(1)} fusion(f32[2,9,640]{1,0,2:T(2,128)S(1)} %copy.85, s32[1024]{0:T(1024)S(1)} %pad_clamp_fusion.6), kind=kCustom, calls=%fused_computation.8.clone | custom fusion | bytes 75776 | tf_op jit(solution)/shard_map/jit(_take)/gather | solution.py:94
  75.8 2.1 %gather_fusion.28 = f32[512,2,9]{2,1,0:T(2,128)S(1)} fusion(f32[2,9,640]{1,0,2:T(2,128)S(1)} %copy.87, s32[1024]{0:T(1024)S(1)} %pad_clamp_fusion.4), kind=kCustom, calls=%fused_computation.9.clone | custom fusion | bytes 75776 | tf_op jit(solution)/shard_map/jit(_take)/gather | solution.py:94
  78.4 2.1 %gather_fusion.29 = f32[512,2,9]{2,1,0:T(2,128)S(1)} fusion(f32[2,9,640]{1,0,2:T(2,128)S(1)} %copy.89, s32[1024]{0:T(1024)S(1)} %pad_clamp_fusion.2), kind=kCustom, calls=%fused_computation.10.clone | custom fusion | bytes 75776 | tf_op jit(solution)/shard_map/jit(_take)/gather | solution.py:94
  81.1 2.1 %gather_fusion.30 = f32[512,2,9]{2,1,0:T(2,128)S(1)} fusion(f32[2,9,640]{1,0,2:T(2,128)S(1)} %copy.91, s32[1024]{0:T(1024)S(1)} %pad_clamp_fusion), kind=kCustom, calls=%fused_computation.11.clone | custom fusion | bytes 75776 | tf_op jit(solution)/shard_map/jit(_take)/gather | solution.py:94
  84.8 2.9 %collective-permute-start.7 = (f32[54,64]{1,0:T(8,128)S(1)}, f32[54,64]{1,0:T(8,128)S(1)}, u32[]{:S(2)}, u32[]{:S(2)}) collective-permute-start(f32[54,64]{1,0:T(8,128)S(1)} %reshape.189), channel_id=1, source_target_pairs={{4,0},{8,4},{12,8},{16,12},{20,16},{24,20},{28,24},{5,1},{9,5},{13... | collective-permute-start | bytes 41480 | tf_op jit(solution)/shard_map/ppermute | solution.py:18
  87.8 3.1 %collective-permute-start.6 = (f32[54,64]{1,0:T(8,128)S(1)}, f32[54,64]{1,0:T(8,128)S(1)}, u32[]{:S(2)}, u32[]{:S(2)}) collective-permute-start(f32[54,64]{1,0:T(8,128)S(1)} %reshape.189), channel_id=1, source_target_pairs={{0,4},{4,8},{8,12},{12,16},{16,20},{20,24},{24,28},{1,5},{5,9},{9,... | collective-permute-start | bytes 41480 | tf_op jit(solution)/shard_map/ppermute | solution.py:18
  91.2 3.2 %collective-permute-done.6 = f32[54,64]{1,0:T(8,128)S(1)} collective-permute-done((f32[54,64]{1,0:T(8,128)S(1)}, f32[54,64]{1,0:T(8,128)S(1)}, u32[]{:S(2)}, u32[]{:S(2)}) %collective-permute-start.6) | collective-permute-done | bytes 13856 | tf_op jit(solution)/shard_map/ppermute | solution.py:18
  98.5 2.1 %gather_fusion.32 = f32[512,2,9]{2,1,0:T(2,128)S(1)} fusion(f32[2,9,640]{1,0,2:T(2,128)S(1)} %copy.98, s32[1024]{0:T(1024)S(1)} %pad_clamp_fusion.8), kind=kCustom, calls=%fused_computation.13.clone | custom fusion | bytes 75776 | tf_op jit(solution)/shard_map/jit(_take)/gather | solution.py:94
  101.2 2.1 %gather_fusion.31 = f32[512,2,9]{2,1,0:T(2,128)S(1)} fusion(f32[2,9,640]{1,0,2:T(2,128)S(1)} %copy.96, s32[1024]{0:T(1024)S(1)} %pad_clamp_fusion.10), kind=kCustom, calls=%fused_computation.12.clone | custom fusion | bytes 75776 | tf_op jit(solution)/shard_map/jit(_take)/gather | solution.py:94
  103.8 2.1 %gather_fusion.33 = f32[512,2,9]{2,1,0:T(2,128)S(1)} fusion(f32[2,9,640]{1,0,2:T(2,128)S(1)} %copy.100, s32[1024]{0:T(1024)S(1)} %pad_clamp_fusion.6), kind=kCustom, calls=%fused_computation.14.clone | custom fusion | bytes 75776 | tf_op jit(solution)/shard_map/jit(_take)/gather | solution.py:94
  106.4 2.1 %gather_fusion.34 = f32[512,2,9]{2,1,0:T(2,128)S(1)} fusion(f32[2,9,640]{1,0,2:T(2,128)S(1)} %copy.102, s32[1024]{0:T(1024)S(1)} %pad_clamp_fusion.4), kind=kCustom, calls=%fused_computation.15.clone | custom fusion | bytes 75776 | tf_op jit(solution)/shard_map/jit(_take)/gather | solution.py:94
  109.0 2.1 %gather_fusion.35 = f32[512,2,9]{2,1,0:T(2,128)S(1)} fusion(f32[2,9,640]{1,0,2:T(2,128)S(1)} %copy.104, s32[1024]{0:T(1024)S(1)} %pad_clamp_fusion.2), kind=kCustom, calls=%fused_computation.16.clone | custom fusion | bytes 75776 | tf_op jit(solution)/shard_map/jit(_take)/gather | solution.py:94
  111.7 2.1 %gather_fusion.36 = f32[512,2,9]{2,1,0:T(2,128)S(1)} fusion(f32[2,9,640]{1,0,2:T(2,128)S(1)} %copy.106, s32[1024]{0:T(1024)S(1)} %pad_clamp_fusion), kind=kCustom, calls=%fused_computation.17.clone | custom fusion | bytes 75776 | tf_op jit(solution)/shard_map/jit(_take)/gather | solution.py:94
  (193 shorter events, 36.2 us)
Async XLA Ops:
  0.0 0.7 copy-start.7
  0.0 0.7 copy-start.8
  2.7 0.7 copy-start.9
  4.3 0.9 copy-start.2
  5.5 0.8 copy-start.3
  6.9 8.9 %copy-start.4 = (s32[6,512]{1,0:T(8,128)S(1)}, s32[6,512]{1,0:T(8,128)}, u32[]{:S(2)}) copy-start(s32[6,512]{1,0:T(8,128)} %param.55) | copy-start | bytes 36868
  6.9 13.7 %collective-permute-start = (f32[136,64]{0,1:T(8,128)S(1)}, f32[136,64]{0,1:T(8,128)S(1)}, u32[]{:S(2)}, u32[]{:S(2)}) collective-permute-start(f32[136,64]{0,1:T(8,128)S(1)} %get-tuple-element.10), channel_id=1, source_target_pairs={{0,1},{1,2},{2,3},{4,5},{5,6},{6,7},{8,9},{9,10},{10,11},{12,13},{... | collective-permute-start | bytes 104456 | tf_op jit(solution)/shard_map/ppermute | solution.py:29
  8.9 11.8 %collective-permute-start.1 = (f32[136,64]{0,1:T(8,128)S(1)}, f32[136,64]{0,1:T(8,128)S(1)}, u32[]{:S(2)}, u32[]{:S(2)}) collective-permute-start(f32[136,64]{0,1:T(8,128)S(1)} %get-tuple-element.11), channel_id=1, source_target_pairs={{1,0},{2,1},{3,2},{5,4},{6,5},{7,6},{9,8},{10,9},{11,10},{13,12},{... | collective-permute-start | bytes 104456 | tf_op jit(solution)/shard_map/ppermute | solution.py:31
  16.0 0.7 copy-start.13
  16.6 0.7 copy-start.12
  17.3 0.7 copy-start.11
  17.9 0.7 copy-start.10
  23.0 5.9 %collective-permute-start.3 = (f32[54,64]{1,0:T(8,128)S(1)}, f32[54,64]{1,0:T(8,128)S(1)}, u32[]{:S(2)}, u32[]{:S(2)}) collective-permute-start(f32[54,64]{1,0:T(8,128)S(1)} %reshape.186), channel_id=1, source_target_pairs={{4,0},{8,4},{12,8},{16,12},{20,16},{24,20},{28,24},{5,1},{9,5},{13... | collective-permute-start | bytes 41480 | tf_op jit(solution)/shard_map/ppermute | solution.py:18
  26.3 6.7 %collective-permute-start.2 = (f32[54,64]{1,0:T(8,128)S(1)}, f32[54,64]{1,0:T(8,128)S(1)}, u32[]{:S(2)}, u32[]{:S(2)}) collective-permute-start(f32[54,64]{1,0:T(8,128)S(1)} %reshape.186), channel_id=1, source_target_pairs={{0,4},{4,8},{8,12},{12,16},{16,20},{20,24},{24,28},{1,5},{5,9},{9,... | collective-permute-start | bytes 41480 | tf_op jit(solution)/shard_map/ppermute | solution.py:18
  52.5 0.8 copy-start.1
  52.5 0.8 copy-start.5
  53.3 0.7 copy-start
  54.3 0.7 copy-start.6
  55.2 6.2 %collective-permute-start.5 = (f32[54,64]{1,0:T(8,128)S(1)}, f32[54,64]{1,0:T(8,128)S(1)}, u32[]{:S(2)}, u32[]{:S(2)}) collective-permute-start(f32[54,64]{1,0:T(8,128)S(1)} %reshape.188), channel_id=1, source_target_pairs={{4,0},{8,4},{12,8},{16,12},{20,16},{24,20},{28,24},{5,1},{9,5},{13... | collective-permute-start | bytes 41480 | tf_op jit(solution)/shard_map/ppermute | solution.py:18
  57.2 6.7 %collective-permute-start.4 = (f32[54,64]{1,0:T(8,128)S(1)}, f32[54,64]{1,0:T(8,128)S(1)}, u32[]{:S(2)}, u32[]{:S(2)}) collective-permute-start(f32[54,64]{1,0:T(8,128)S(1)} %reshape.188), channel_id=1, source_target_pairs={{0,4},{4,8},{8,12},{12,16},{16,20},{20,24},{24,28},{1,5},{5,9},{9,... | collective-permute-start | bytes 41480 | tf_op jit(solution)/shard_map/ppermute | solution.py:18
  84.8 6.3 %collective-permute-start.7 = (f32[54,64]{1,0:T(8,128)S(1)}, f32[54,64]{1,0:T(8,128)S(1)}, u32[]{:S(2)}, u32[]{:S(2)}) collective-permute-start(f32[54,64]{1,0:T(8,128)S(1)} %reshape.189), channel_id=1, source_target_pairs={{4,0},{8,4},{12,8},{16,12},{20,16},{24,20},{28,24},{5,1},{9,5},{13... | collective-permute-start | bytes 41480 | tf_op jit(solution)/shard_map/ppermute | solution.py:18
  87.8 6.7 %collective-permute-start.6 = (f32[54,64]{1,0:T(8,128)S(1)}, f32[54,64]{1,0:T(8,128)S(1)}, u32[]{:S(2)}, u32[]{:S(2)}) collective-permute-start(f32[54,64]{1,0:T(8,128)S(1)} %reshape.189), channel_id=1, source_target_pairs={{0,4},{4,8},{8,12},{12,16},{16,20},{20,24},{24,28},{1,5},{5,9},{9,... | collective-permute-start | bytes 41480 | tf_op jit(solution)/shard_map/ppermute | solution.py:18
where the time goes:
time: 117 us; the launch traced here: 116 us
  local copies, waits for them, and re-layouts  71.4 us (61%)
  starting transfers between devices  23.5 us (20%)
  waiting for transfers between devices  9.71 us (8%)
  other arithmetic  6.11 us (5%)
  between operations  3.84 us (3%)
  matrix products  1.58 us (1%)
    gather x36, local copies, waits for them, and re-layouts, laplace_part(): picked = jnp.take(face_rows, clamped, axis=2)  41.1 us
    ppermute x6, starting transfers between devices, from_behind(): return lax.ppermute(block, axis, route)  17.9 us
    gather x36, local copies, waits for them, and re-layouts, laplace_part(): face_rows = extended[:, across[surface]]  16.4 us
    ppermute x6, waiting for transfers between devices, from_behind(): return lax.ppermute(block, axis, route)  9.71 us
    unnamed x31, local copies, waits for them, and re-layouts  7.66 us
    ppermute x1, starting transfers between devices, extended_2(): lax.ppermute(head, axis, [((i + 1) % count, i) for i in range(ends)])  3.64 us
  transfers between devices with their start and end apart: 8, of which 3 were waited for; matrix products, arithmetic and copies ran while one was open for 4% of the time, Pallas kernels for 0%

commit v1 on v0

v1 whole, which is shorter than its diff:
```python
import functools

import jax
import jax.numpy as jnp
import numpy as np
from jax import lax
from jax.experimental import pallas as pl
from jax.experimental.pallas import tpu as pltpu
from jax.sharding import PartitionSpec as P

SWEEPS = 3
MESH = pl.DeviceIdType.MESH
F32 = jnp.float32
BF16 = jnp.bfloat16
LANES = 128
HALF = 64
ROWS = 32
FACE_ROWS = 112

time_step = 0.01
gradient_energy = 0.01
penalty = 2.0


def element_tables():
    weights = np.array([0.5, 2.0, 0.5])
    slope_table = np.array([[7.0, -8.0, 1.0], [-8.0, 16.0, -8.0], [1.0, -8.0, 7.0]])
    diagonal = np.diag(weights)
    stiffness = (
        np.kron(slope_table, np.kron(diagonal, diagonal))
        + np.kron(diagonal, np.kron(slope_table, diagonal))
        + np.kron(diagonal, np.kron(diagonal, slope_table))
    )
    mass_table = np.kron(weights, np.kron(weights, weights))
    face_diag = np.zeros(27)
    select = np.zeros((FACE_ROWS, 2 * ROWS))
    scatter = np.zeros((2 * ROWS, FACE_ROWS))
    for direction in range(3):
        for side in range(2):
            surface = 2 * direction + side
            for major in range(3):
                for minor in range(3):
                    near = [major, minor]
                    near.insert(direction, 2 * side)
                    far = [major, minor]
                    far.insert(direction, 2 - 2 * side)
                    near_node = near[0] * 9 + near[1] * 3 + near[2]
                    far_node = far[0] * 9 + far[1] * 3 + far[2]
                    weight = weights[major] * weights[minor]
                    face_diag[near_node] += weight
                    for part in range(2):
                        row = surface * 18 + part * 9 + major * 3 + minor
                        select[row, part * ROWS + far_node] = -6.0 * penalty * weight
                        scatter[part * ROWS + near_node, row] = 1.0
    block = stiffness + 6.0 * penalty * np.diag(face_diag)
    local = np.zeros((2 * ROWS, 2 * ROWS))
    local[:27, :27] = block
    local[ROWS : ROWS + 27, ROWS : ROWS + 27] = block
    first = np.concatenate([local, select], 0)
    first = np.concatenate([first, first], 1)
    second = np.concatenate([scatter, scatter], 1)
    inverse = np.zeros((ROWS, LANES))
    inverse[:27] = 1.0 / mass_table[:, None]
    return first, second, inverse


def split(values):
    high = values.astype(BF16)
    low = (values - high.astype(F32)).astype(BF16)
    return jnp.concatenate([high, low], 0)


def kernel(
    n_seg, n_sub, old_cuts, new_cuts, start, right, prev, refined, links, first, second, inverse,
    out, fields, flags, link_buf, first_buf, second_buf, inverse_buf,
    index_buf, block_buf, head_out, tail_out, head_in, tail_in, ghost_out, ghost_in,
    moved_buf, face_buf, load_sem, head_sem, tail_sem, ghost_send, ghost_recv,
):
    seg, sub = lax.axis_index("seg"), lax.axis_index("sub")
    capacity = links.shape[1]
    blocks = capacity // LANES

    loads = [
        pltpu.make_async_copy(source, target, load_sem.at[i])
        for i, (source, target) in enumerate(
            [
                (start, fields.at[pl.ds(0, 2)]),
                (right, fields.at[pl.ds(2, 2)]),
                (prev, fields.at[4]),
                (refined, flags),
                (links, link_buf),
                (first, first_buf),
                (second, second_buf),
                (inverse, inverse_buf),
            ]
        )
    ]
    for load in loads:
        load.start()

    head_in[...] = jnp.zeros_like(head_in)
    tail_in[...] = jnp.zeros_like(tail_in)
    ghost_in[...] = jnp.zeros_like(ghost_in)

    left = (sub > 0, (seg, sub - 1))
    after = (sub < n_sub - 1, (seg, sub + 1))
    below = (seg > 0, (seg - 1, sub))
    above = (seg < n_seg - 1, (seg + 1, sub))
    sides = (left, after, below, above)
    barrier = pltpu.get_barrier_semaphore()
    for there, place in sides:
        @pl.when(there)
        def _(place=place):
            pl.semaphore_signal(barrier, inc=1, device_id=place, device_id_type=MESH)

    head_copy = pltpu.make_async_remote_copy(
        src_ref=head_out, dst_ref=head_in, send_sem=head_sem.at[0], recv_sem=head_sem.at[1],
        device_id=left[1], device_id_type=MESH)
    tail_copy = pltpu.make_async_remote_copy(
        src_ref=tail_out, dst_ref=tail_in, send_sem=tail_sem.at[0], recv_sem=tail_sem.at[1],
        device_id=after[1], device_id_type=MESH)
    up_copies, down_copies = [], []
    for sweep in range(SWEEPS):
        up_copies.append(pltpu.make_async_remote_copy(
            src_ref=ghost_out.at[sweep], dst_ref=ghost_in.at[sweep, 0],
            send_sem=ghost_send.at[sweep, 0], recv_sem=ghost_recv.at[sweep, 0],
            device_id=above[1], device_id_type=MESH))
        down_copies.append(pltpu.make_async_remote_copy(
            src_ref=ghost_out.at[sweep], dst_ref=ghost_in.at[sweep, 1],
            send_sem=ghost_send.at[sweep, 1], recv_sem=ghost_recv.at[sweep, 1],
            device_id=below[1], device_id_type=MESH))

    old_first, old_end = old_cuts[0, sub], old_cuts[0, sub + 1]
    new_first, new_end = new_cuts[0, sub], new_cuts[0, sub + 1]
    left_first = old_cuts[0, jnp.maximum(sub - 1, 0)]
    old_count, new_count = old_end - old_first, new_end - new_first
    shift = new_first - old_first
    mask = LANES - 1
    lane = lax.broadcasted_iota(jnp.int32, (8, LANES), 1)
    row = lax.broadcasted_iota(jnp.int32, (8, LANES), 0)

    def wide(values, rows):
        return jnp.broadcast_to(values[:1], (rows, LANES))

    def lanes(rows):
        return lax.broadcasted_iota(jnp.int32, (rows, LANES), 1)

    for i in range(4):
        loads[i].wait()

    pad = jnp.zeros((ROWS - 27, LANES), F32)
    row32 = lax.broadcasted_iota(jnp.int32, (ROWS, LANES), 0)

    def packed(b):
        cols = pl.ds(b * LANES, LANES)
        parts = [jnp.concatenate([fields[g, :, cols], pad], 0) for g in range(5)]
        flag = flags[:, cols].astype(F32)
        parts[4] = jnp.where(row32 == 27, jnp.broadcast_to(flag, (ROWS, LANES)), parts[4])
        return jnp.concatenate(parts, 0)

    all_rows = 5 * ROWS
    upper = all_rows // 2
    whole = [packed(b) for b in range(blocks)]
    lane_u = lanes(upper)
    head_out[...] = jnp.where(lane_u < HALF, whole[0][:upper], pltpu.roll(whole[0][upper:], HALF, 1))
    tail = whole[0]
    lane_a = lanes(all_rows)
    window = (lane_u >= old_count - HALF) & (lane_u < old_count)
    for b in range(1, blocks):
        slot = lane_a + b * LANES
        inside = (slot >= old_count - HALF) & (slot < old_count)
        tail = jnp.where(inside, whole[b], tail)
        slot_u = lane_u + b * LANES
        window = window | ((slot_u >= old_count - HALF) & (slot_u < old_count))
    tail_out[...] = jnp.where(window, tail[:upper], pltpu.roll(tail[upper:], HALF, 1))

    pl.semaphore_wait(
        barrier,
        (jnp.minimum(sub, 1) + jnp.minimum(n_sub - 1 - sub, 1)
         + jnp.minimum(seg, 1) + jnp.minimum(n_seg - 1 - seg, 1)),
    )

    @pl.when(after[0])
    def _():
        tail_copy.start()

    @pl.when(left[0])
    def _():
        head_copy.start()

    turn = (-shift) & mask
    turned = [pltpu.roll(w, turn, 1) for w in whole]
    came_from = lane_a + shift
    for b in range(blocks):
        mine = turned[b]
        if b > 0:
            mine = jnp.where(came_from < 0, turned[b - 1], mine)
        if b < blocks - 1:
            mine = jnp.where(came_from >= LANES, turned[b + 1], mine)
        moved_buf[:, b * LANES : (b + 1) * LANES] = mine

    loads[4].wait()
    for b in range(blocks):
        cols = pl.ds(b * LANES, LANES)
        rows = [jnp.broadcast_to(link_buf[f : f + 1, cols], (8, LANES)) for f in range(6)]
        parts = []
        for k in range(FACE_ROWS // 8):
            f0, f1 = min(8 * k // 18, 5), min((8 * k + 7) // 18, 5)
            part = rows[f0]
            if f1 != f0:
                part = jnp.where(row < f1 * 18 - 8 * k, part, rows[f1])
            parts.append(part)
        link = jnp.concatenate(parts, 0)
        index_buf[:, cols] = link & mask
        block_buf[:, cols] = link >> 7
    for i in range(5, 8):
        loads[i].wait()

    @pl.when(left[0])
    def _():
        tail_copy.wait_recv()

    offset = left_first - new_first
    from_left = jnp.concatenate(
        [
            pltpu.roll(tail_in[...], offset & mask, 1),
            pltpu.roll(tail_in[...], (offset + HALF) & mask, 1),
        ],
        0,
    )
    block0 = jnp.where(lane_a < -shift, from_left, moved_buf[:, :LANES])
    block0 = jnp.where(lane_a < new_count, block0, 0.0)

    def send(sweep, c, mu):
        lane32 = lanes(ROWS)
        ghost_out[sweep] = jnp.where(lane32 < HALF, c, pltpu.roll(mu, HALF, 1))

        @pl.when(above[0])
        def _():
            up_copies[sweep].start()

        @pl.when(below[0])
        def _():
            down_copies[sweep].start()

    send(0, block0[:ROWS], block0[ROWS : 2 * ROWS])
    moved_buf[:, :LANES] = block0

    @pl.when(after[0])
    def _():
        head_copy.wait_recv()

    edge = old_end - new_first
    from_right = jnp.concatenate(
        [
            pltpu.roll(head_in[...], edge & mask, 1),
            pltpu.roll(head_in[...], (edge + HALF) & mask, 1),
        ],
        0,
    )
    state, coefficients = [], []
    inverse_mass = inverse_buf[...]
    for b in range(blocks):
        slot = lane_a + b * LANES
        whole_b = moved_buf[:, b * LANES : (b + 1) * LANES]
        whole_b = jnp.where(slot >= edge, from_right, whole_b)
        whole_b = jnp.where(slot < new_count, whole_b, 0.0)
        state.append(whole_b[: 2 * ROWS])
        prior = whole_b[4 * ROWS :]
        flag = jnp.broadcast_to(prior[27:28], (ROWS, LANES))
        inverse_lumped = inverse_mass * (1.0 + 7.0 * flag)
        stiff = (1.0 - 0.5 * flag) * inverse_lumped * (1.0 / 6.0)
        coefficients.append(
            (
                whole_b[2 * ROWS : 3 * ROWS] * inverse_lumped,
                whole_b[3 * ROWS : 4 * ROWS] * inverse_lumped,
                time_step * stiff * (1.0 - prior * prior),
                gradient_energy * stiff,
                3.0 * prior * prior - 1.0,
            )
        )

    spread_ratio = 2.0
    half_width = 0.5
    weight_prev = 1.0 / spread_ratio
    update = [None] * blocks
    first_table, second_table = first_buf[...], second_buf[...]
    lane32 = lanes(ROWS)
    for sweep in range(SWEEPS):
        last = sweep == SWEEPS - 1
        product = jnp.dot(
            first_table, jnp.concatenate([split(v) for v in state], 1), preferred_element_type=F32
        )
        near = product[: 2 * ROWS]
        sources = [product[2 * ROWS :, b * LANES : (b + 1) * LANES] for b in range(blocks)]

        def pick(total, source, number, b):
            cols = slice(b * LANES, (b + 1) * LANES)
            index = index_buf[:, cols]
            got = jnp.take_along_axis(source, index, axis=1, mode="promise_in_bounds")
            return jnp.where(block_buf[:, cols] == number, got, total)

        faces = []
        for b in range(blocks):
            total = jnp.zeros((FACE_ROWS, LANES), F32)
            for number in range(blocks):
                total = pick(total, sources[number], number, b)
            faces.append(total)

        @pl.when(below[0])
        def _():
            up_copies[sweep].wait_recv()

        @pl.when(above[0])
        def _():
            down_copies[sweep].wait_recv()

        got_below, got_above = ghost_in[sweep, 0], ghost_in[sweep, 1]
        ghost = jnp.concatenate(
            [
                jnp.where(lane32 < HALF, got_below, pltpu.roll(got_above, HALF, 1)),
                jnp.where(lane32 < HALF, pltpu.roll(got_below, HALF, 1), got_above),
            ],
            0,
        )
        ghost_faces = jnp.dot(first_table[2 * ROWS :], split(ghost), preferred_element_type=F32)

        weight_now = 1.0 / (2.0 * spread_ratio - weight_prev)
        for b in range(blocks):
            total = pick(faces[b], ghost_faces, blocks, b)
            coupled = jnp.dot(second_table, split(total), preferred_element_type=F32)
            laplace = near[:, b * LANES : (b + 1) * LANES] + coupled
            side_c, side_mu, mobile, stiff, curvature = coefficients[b]
            c, mu = state[b][:ROWS], state[b][ROWS:]
            scaled = jnp.concatenate(
                [
                    side_c - c - mobile * laplace[ROWS:],
                    side_mu - mu + curvature * c + stiff * laplace[:ROWS],
                ],
                0,
            )
            if sweep == 0:
                update[b] = scaled
            else:
                update[b] = (
                    weight_now * weight_prev * update[b] + (2.0 * weight_now / half_width) * scaled
                )
            state[b] = state[b] + update[b]
            if last:
                cols = pl.ds(b * LANES, LANES)
                out[0, :, cols] = state[b][:27]
                out[1, :, cols] = state[b][ROWS : ROWS + 27]
            elif b == 0:
                send(sweep + 1, state[0][:ROWS], state[0][ROWS:])
        if sweep > 0:
            weight_prev = weight_now

    @pl.when(left[0])
    def _():
        head_copy.wait_send()

    @pl.when(after[0])
    def _():
        tail_copy.wait_send()

    for sweep in range(SWEEPS):
        @pl.when(above[0])
        def _():
            up_copies[sweep].wait_send()

        @pl.when(below[0])
        def _():
            down_copies[sweep].wait_send()


def local(n_seg, n_sub, start_state, right_side, previous, refined, old_cuts, new_cuts, face_links):
    capacity = start_state.shape[-1]
    first, second, inverse = element_tables()
    any_space = pl.BlockSpec(memory_space=pl.ANY)
    smem = pl.BlockSpec(memory_space=pltpu.SMEM)
    packed_rows = 5 * ROWS // 2
    return pl.pallas_call(
        functools.partial(kernel, n_seg, n_sub),
        out_shape=jax.ShapeDtypeStruct((2, 27, capacity), F32),
        in_specs=[smem, smem] + [any_space] * 8,
        out_specs=pl.BlockSpec(memory_space=pltpu.VMEM),
        scratch_shapes=[
            pltpu.VMEM((5, 27, capacity), F32),
            pltpu.VMEM((1, capacity), jnp.int32),
            pltpu.VMEM((6, capacity), jnp.int32),
            pltpu.VMEM(first.shape, BF16),
            pltpu.VMEM(second.shape, BF16),
            pltpu.VMEM(inverse.shape, F32),
            pltpu.VMEM((FACE_ROWS, capacity), jnp.int32),
            pltpu.VMEM((FACE_ROWS, capacity), jnp.int32),
            pltpu.VMEM((packed_rows, LANES), F32),
            pltpu.VMEM((packed_rows, LANES), F32),
            pltpu.VMEM((packed_rows, LANES), F32),
            pltpu.VMEM((packed_rows, LANES), F32),
            pltpu.VMEM((SWEEPS, ROWS, LANES), F32),
            pltpu.VMEM((SWEEPS, 2, ROWS, LANES), F32),
            pltpu.VMEM((5 * ROWS, capacity), F32),
            pltpu.VMEM((8, LANES), F32),
            pltpu.SemaphoreType.DMA((8,)),
            pltpu.SemaphoreType.DMA((2,)),
            pltpu.SemaphoreType.DMA((2,)),
            pltpu.SemaphoreType.DMA((SWEEPS, 2)),
            pltpu.SemaphoreType.DMA((SWEEPS, 2)),
        ],
        compiler_params=pltpu.CompilerParams(
            collective_id=0, has_side_effects=True, vmem_limit_bytes=16 * 1024 * 1024
        ),
        name="smooth",
    )(
        old_cuts, new_cuts, start_state, right_side, previous, refined.reshape(1, capacity),
        face_links, jnp.asarray(first, BF16), jnp.asarray(second, BF16), jnp.asarray(inverse, F32),
    )


def solution(mesh):
    placed = (
        P(None, None, ("seg", "sub")),
        P(None, None, ("seg", "sub")),
        P(None, ("seg", "sub")),
        P(("seg", "sub")),
        P("seg", None),
        P("seg", None),
        P(None, ("seg", "sub")),
    )
    return jax.shard_map(
        functools.partial(local, mesh.shape["seg"], mesh.shape["sub"]),
        mesh=mesh, in_specs=placed, out_specs=P(None, None, ("seg", "sub")), check_vma=False,
    )
```

time: 117 us -> 19.2 us (0.16)
  the two profiles are of different devices: /device:TPU:20 before, /device:TPU:0 now
where the time goes in v1:
time: 19.2 us; the launch traced here: 19 us
  Pallas kernels  16.4 us (85%)
  local copies, waits for them, and re-layouts  2.47 us (13%)
    pallas_call x1, Pallas kernels, local(): pl.pallas_call(functools.partial(kernel, n_seg, n_sub), out_shape=jax.Sha...  16.4 us
    unnamed x20, local copies, waits for them, and re-layouts  1.74 us
    pallas_call x1, local copies, waits for them, and re-layouts, local(): pl.pallas_call(functools.partial(kernel, n_seg, n_sub), out_shape=jax.Sha...  0.73 us

profile of v1, /device:TPU:0, one launch (start us, length us, event | category | flops | bytes accessed | tf_op | source)
XLA Modules:
  0.0 19.0 jit_solution(15133895216426410977)
XLA Ops:
  0.0 0.0 copy-start.8
  0.0 1.0 %copy.11.start = f32[2,27,512]{2,1,0:T(8,128)S(1)} copy(f32[2,27,512]{2,0,1:T(2,128)} %param.10) | data formatting | bytes 221184 | tf_op args[0]
  1.0 0.0 copy-done.8
  1.0 0.0 copy-start
  1.0 0.0 copy-start.1
  1.0 0.0 copy-start.2
  1.0 0.0 copy-start.3
  1.0 0.0 copy-start.4
  1.0 0.0 copy-start.5
  1.0 0.0 copy-start.6
  1.1 0.0 copy-start.7
  1.1 0.7 %copy-done = f32[27,512]{1,0:T(8,128)S(1)} copy-done((f32[27,512]{1,0:T(8,128)S(1)}, f32[27,512]{1,0:T(8,128)}, u32[]{:S(2)}) %copy-start) | copy-done | bytes 55320
  1.8 0.0 copy-done.1
  1.8 0.0 copy-done.2
  1.8 0.0 copy-done.3
  1.8 0.0 copy-done.4
  1.8 0.0 copy-done.5
  1.8 0.0 copy-done.6
  1.8 0.0 copy-done.7
  1.9 16.4 %smooth.1 = f32[2,27,512]{2,1,0:T(8,128)S(1)} custom-call(s32[1,5]{1,0:T(1,128)S(1)} %copy-done.6, s32[1,5]{1,0:T(1,128)S(1)} %copy-done.7, f32[2,27,512]{2,1,0:T(8,128)S(1)} %copy.11.start, f32[2,27,512]{2,1,0:T(8,128)S(1)} %copy.12.right, f32[27,512]{1,0:T(8,128)S(1)} %copy-done, s32[1,512]{1,0:T(1,128)S(1)} %bitcast.1, s32[6,512]{1,0:T(8,128)S(1)} %copy-done.3, ...), custom_call_target="tpu_custom_call" | custom-call | tf_op jit(solution)/shard_map/smooth/pallas_call | solution.py:382
  18.3 0.7 %copy.13 = f32[2,27,512]{2,0,1:T(2,128)} copy(f32[2,27,512]{2,1,0:T(8,128)S(1)} %smooth.1) | data formatting | bytes 221184 | tf_op jit(solution)/shard_map/smooth/pallas_call | solution.py:382
  (1 shorter events, 0.0 us)
Async XLA Ops:
  0.0 1.0 %copy-start.8 = (f32[2,27,512]{2,0,1:T(2,128)S(1)}, f32[2,27,512]{2,0,1:T(2,128)}, u32[]{:S(2)}) copy-start(f32[2,27,512]{2,0,1:T(2,128)} %param.11) | copy-start | bytes 331780
  1.0 0.8 %copy-start = (f32[27,512]{1,0:T(8,128)S(1)}, f32[27,512]{1,0:T(8,128)}, u32[]{:S(2)}) copy-start(f32[27,512]{1,0:T(8,128)} %prev.1) | copy-start | bytes 165892
  1.0 0.8 %copy-start.1 = (bf16[176,128]{1,0:T(8,128)(2,1)S(1)}, bf16[176,128]{1,0:T(8,128)(2,1)}, u32[]{:S(2)}) copy-start(bf16[176,128]{1,0:T(8,128)(2,1)} %constant.6.clone.first) | copy-start | bytes 135172
  1.0 0.8 %copy-start.2 = (bf16[64,224]{1,0:T(8,128)(2,1)S(1)}, bf16[64,224]{1,0:T(8,128)(2,1)}, u32[]{:S(2)}) copy-start(bf16[64,224]{1,0:T(8,128)(2,1)} %constant.7.clone.second) | copy-start | bytes 86020
  1.0 0.8 %copy-start.3 = (s32[6,512]{1,0:T(8,128)S(1)}, s32[6,512]{1,0:T(8,128)}, u32[]{:S(2)}) copy-start(s32[6,512]{1,0:T(8,128)} %links.1) | copy-start | bytes 36868
  1.0 0.8 %copy-start.4 = (f32[32,128]{1,0:T(8,128)S(1)}, f32[32,128]{1,0:T(8,128)}, u32[]{:S(2)}) copy-start(f32[32,128]{1,0:T(8,128)} %constant.8.clone.inverse) | copy-start | bytes 49156
  1.0 0.8 %copy-start.5 = (s32[512]{0:T(512)S(1)}, s32[512]{0:T(512)}, u32[]{:S(2)}) copy-start(s32[512]{0:T(512)} %param.13) | copy-start | bytes 6148
  1.0 0.8 %copy-start.6 = (s32[1,5]{1,0:T(1,128)S(1)}, s32[1,5]{1,0:T(1,128)}, u32[]{:S(2)}) copy-start(s32[1,5]{1,0:T(1,128)} %old_cuts.1) | copy-start | bytes 64
  1.1 0.8 %copy-start.7 = (s32[1,5]{1,0:T(1,128)S(1)}, s32[1,5]{1,0:T(1,128)}, u32[]{:S(2)}) copy-start(s32[1,5]{1,0:T(1,128)} %new_cuts.1) | copy-start | bytes 64

commit v2 on v1

--- a/solution.py
+++ b/solution.py
@@ -72,7 +72,7 @@
 
 def kernel(
     n_seg, n_sub, old_cuts, new_cuts, start, right, prev, refined, links, first, second, inverse,
-    out, fields, flags, link_buf, first_buf, second_buf, inverse_buf,
+    out, state_buf, side_buf, prior_buf, flags, link_buf, first_buf, second_buf, inverse_buf,
     index_buf, block_buf, head_out, tail_out, head_in, tail_in, ghost_out, ghost_in,
     moved_buf, face_buf, load_sem, head_sem, tail_sem, ghost_send, ghost_recv,
 ):
@@ -84,9 +84,9 @@
         pltpu.make_async_copy(source, target, load_sem.at[i])
         for i, (source, target) in enumerate(
             [
-                (start, fields.at[pl.ds(0, 2)]),
-                (right, fields.at[pl.ds(2, 2)]),
-                (prev, fields.at[4]),
+                (start, state_buf),
+                (right, side_buf),
+                (prev, prior_buf),
                 (refined, flags),
                 (links, link_buf),
                 (first, first_buf),
@@ -153,7 +153,16 @@
 
     def packed(b):
         cols = pl.ds(b * LANES, LANES)
-        parts = [jnp.concatenate([fields[g, :, cols], pad], 0) for g in range(5)]
+        parts = [
+            jnp.concatenate([rows, pad], 0)
+            for rows in (
+                state_buf[pl.ds(2 * b, 27, stride=2 * blocks), :],
+                state_buf[pl.ds(2 * b + 1, 27, stride=2 * blocks), :],
+                side_buf[pl.ds(2 * b, 27, stride=2 * blocks), :],
+                side_buf[pl.ds(2 * b + 1, 27, stride=2 * blocks), :],
+                prior_buf[:, cols],
+            )
+        ]
         flag = flags[:, cols].astype(F32)
         parts[4] = jnp.where(row32 == 27, jnp.broadcast_to(flag, (ROWS, LANES)), parts[4])
         return jnp.concatenate(parts, 0)
@@ -347,9 +356,8 @@
                 )
             state[b] = state[b] + update[b]
             if last:
-                cols = pl.ds(b * LANES, LANES)
-                out[0, :, cols] = state[b][:27]
-                out[1, :, cols] = state[b][ROWS : ROWS + 27]
+                out[pl.ds(2 * b, 27, stride=2 * blocks), :] = state[b][:27]
+                out[pl.ds(2 * b + 1, 27, stride=2 * blocks), :] = state[b][ROWS : ROWS + 27]
             elif b == 0:
                 send(sweep + 1, state[0][:ROWS], state[0][ROWS:])
         if sweep > 0:
@@ -379,13 +387,21 @@
     any_space = pl.BlockSpec(memory_space=pl.ANY)
     smem = pl.BlockSpec(memory_space=pltpu.SMEM)
     packed_rows = 5 * ROWS // 2
-    return pl.pallas_call(
+    blocks = capacity // LANES
+
+    def by_node(array):
+        array = array.transpose(1, 0, 2).reshape(27, 2, blocks, LANES)
+        return array.transpose(0, 2, 1, 3).reshape(54 * blocks, LANES)
+
+    smoothed = pl.pallas_call(
         functools.partial(kernel, n_seg, n_sub),
-        out_shape=jax.ShapeDtypeStruct((2, 27, capacity), F32),
+        out_shape=pltpu.VMEM((54 * blocks, LANES), F32),
         in_specs=[smem, smem] + [any_space] * 8,
         out_specs=pl.BlockSpec(memory_space=pltpu.VMEM),
         scratch_shapes=[
-            pltpu.VMEM((5, 27, capacity), F32),
+            pltpu.VMEM((54 * blocks, LANES), F32),
+            pltpu.VMEM((54 * blocks, LANES), F32),
+            pltpu.VMEM((27, capacity), F32),
             pltpu.VMEM((1, capacity), jnp.int32),
             pltpu.VMEM((6, capacity), jnp.int32),
             pltpu.VMEM(first.shape, BF16),
@@ -408,13 +424,16 @@
             pltpu.SemaphoreType.DMA((SWEEPS, 2)),
         ],
         compiler_params=pltpu.CompilerParams(
-            collective_id=0, has_side_effects=True, vmem_limit_bytes=16 * 1024 * 1024
+            collective_id=0, has_side_effects=True, vmem_limit_bytes=60 * 1024 * 1024
         ),
         name="smooth",
     )(
-        old_cuts, new_cuts, start_state, right_side, previous, refined.reshape(1, capacity),
+        old_cuts, new_cuts, by_node(start_state), by_node(right_side), previous,
+        refined.reshape(1, capacity),
         face_links, jnp.asarray(first, BF16), jnp.asarray(second, BF16), jnp.asarray(inverse, F32),
     )
+    smoothed = smoothed.reshape(27, blocks, 2, LANES).transpose(2, 0, 1, 3)
+    return smoothed.reshape(2, 27, capacity)
 
 
 def solution(mesh):

time: 19.2 us -> 16.8 us (0.88)
  local copies, waits for them, and re-layouts: 2.47 us -> 0.65 us
  Pallas kernels: 16.4 us -> 16 us
    unnamed x20 -> x1, local copies, waits for them, and re-layouts: 1.74 us -> 0.65 us
    pallas_call x1 -> x0, local copies, waits for them, and re-layouts: 0.73 us -> none  [local(): pl.pallas_call(functools.partial(kernel, n_seg, n_sub), out_shape=jax.Sha...]
    pallas_call x1, Pallas kernels: 16.4 us -> 16 us  [local(): pl.pallas_call(functools.partial(kernel, n_seg, n_sub), out_shape=pltpu.V...]
where the time goes in v2:
time: 16.8 us; the launch traced here: 16.6 us
  Pallas kernels  16 us (95%)
  local copies, waits for them, and re-layouts  0.65 us (4%)
    pallas_call x1, Pallas kernels, local(): pl.pallas_call(functools.partial(kernel, n_seg, n_sub), out_shape=pltpu.V...  16 us
    unnamed x1, local copies, waits for them, and re-layouts  0.65 us

profile of v2, /device:TPU:0, one launch (start us, length us, event | category | flops | bytes accessed | tf_op | source)
XLA Modules:
  0.0 16.6 jit_solution(90246947200728709)
XLA Ops:
  0.0 16.0 %smooth.1 = f32[216,128]{1,0:T(8,128)S(1)} custom-call(s32[1,5]{1,0:T(1,128)} %old_cuts.1, s32[1,5]{1,0:T(1,128)} %new_cuts.1, f32[216,128]{1,0:T(8,128)} %bitcast.21, f32[216,128]{1,0:T(8,128)} %bitcast.22, f32[27,512]{1,0:T(8,128)} %prev.1, s32[1,512]{1,0:T(1,128)} %bitcast.23, s32[6,512]{1,0:T(8,128)} %links.1, bf16[176,128]{1,0:T(8,128)(2,1)} %constant.6.clone.first, ...), custom_call_target="tpu_custom_call" | custom-call | tf_op jit(solution)/shard_map/smooth/pallas_call | solution.py:396
  16.0 0.6 %copy.15 = f32[2,27,512]{2,0,1:T(2,128)} copy(f32[2,27,512]{2,0,1:T(2,128)S(1)} %bitcast.20) | data formatting | bytes 221184

commit v3 on v2

--- a/solution.py
+++ b/solution.py
@@ -74,7 +74,8 @@
     n_seg, n_sub, old_cuts, new_cuts, start, right, prev, refined, links, first, second, inverse,
     out, state_buf, side_buf, prior_buf, flags, link_buf, first_buf, second_buf, inverse_buf,
     index_buf, block_buf, head_out, tail_out, head_in, tail_in, ghost_out, ghost_in,
-    moved_buf, face_buf, load_sem, head_sem, tail_sem, ghost_send, ghost_recv,
+    corner_out, corner_in, moved_buf, load_sem, head_sem, tail_sem, ghost_send, ghost_recv,
+    corner_send, corner_recv,
 ):
     seg, sub = lax.axis_index("seg"), lax.axis_index("sub")
     capacity = links.shape[1]
@@ -101,12 +102,17 @@
     head_in[...] = jnp.zeros_like(head_in)
     tail_in[...] = jnp.zeros_like(tail_in)
     ghost_in[...] = jnp.zeros_like(ghost_in)
+    corner_in[...] = jnp.zeros_like(corner_in)
 
     left = (sub > 0, (seg, sub - 1))
     after = (sub < n_sub - 1, (seg, sub + 1))
     below = (seg > 0, (seg - 1, sub))
     above = (seg < n_seg - 1, (seg + 1, sub))
-    sides = (left, after, below, above)
+    above_after = (above[0] & after[0], (seg + 1, sub + 1))
+    below_after = (below[0] & after[0], (seg - 1, sub + 1))
+    above_left = (above[0] & left[0], (seg + 1, sub - 1))
+    below_left = (below[0] & left[0], (seg - 1, sub - 1))
+    sides = (left, after, below, above, above_left, below_left)
     barrier = pltpu.get_barrier_semaphore()
     for there, place in sides:
         @pl.when(there)
@@ -130,6 +136,13 @@
             send_sem=ghost_send.at[sweep, 1], recv_sem=ghost_recv.at[sweep, 1],
             device_id=below[1], device_id_type=MESH))
 
+    corner_up = pltpu.make_async_remote_copy(
+        src_ref=corner_out, dst_ref=corner_in.at[0], send_sem=corner_send.at[0],
+        recv_sem=corner_recv.at[0], device_id=above_after[1], device_id_type=MESH)
+    corner_down = pltpu.make_async_remote_copy(
+        src_ref=corner_out, dst_ref=corner_in.at[1], send_sem=corner_send.at[1],
+        recv_sem=corner_recv.at[1], device_id=below_after[1], device_id_type=MESH)
+
     old_first, old_end = old_cuts[0, sub], old_cuts[0, sub + 1]
     new_first, new_end = new_cuts[0, sub], new_cuts[0, sub + 1]
     left_first = old_cuts[0, jnp.maximum(sub - 1, 0)]
@@ -183,11 +196,28 @@
         window = window | ((slot_u >= old_count - HALF) & (slot_u < old_count))
     tail_out[...] = jnp.where(window, tail[:upper], pltpu.roll(tail[upper:], HALF, 1))
 
-    pl.semaphore_wait(
-        barrier,
-        (jnp.minimum(sub, 1) + jnp.minimum(n_sub - 1 - sub, 1)
-         + jnp.minimum(seg, 1) + jnp.minimum(n_seg - 1 - seg, 1)),
-    )
+    turn = (-shift) & mask
+    lane32 = lanes(ROWS)
+    slot32 = lane32 & (HALF - 1)
+
+    def both(rows, amount):
+        return jnp.where(
+            lane32 < HALF,
+            pltpu.roll(rows[:ROWS], amount & mask, 1),
+            pltpu.roll(rows[ROWS : 2 * ROWS], (amount + HALF) & mask, 1),
+        )
+
+    ghost_out[0] = jnp.where(
+        (slot32 >= -shift) & (slot32 < new_count), both(whole[0], turn), 0.0
+    )
+    next_count = new_cuts[0, jnp.minimum(sub + 2, n_sub)] - new_end
+    corner_out[...] = jnp.where(
+        (slot32 < old_end - new_end) & (slot32 < next_count), both(tail, old_first - new_end), 0.0
+    )
+
+    seg_sides = jnp.minimum(seg, 1) + jnp.minimum(n_seg - 1 - seg, 1)
+    has_after = jnp.minimum(n_sub - 1 - sub, 1)
+    pl.semaphore_wait(barrier, jnp.minimum(sub, 1) + has_after + seg_sides * (1 + has_after))
 
     @pl.when(after[0])
     def _():
@@ -197,7 +227,14 @@
     def _():
         head_copy.start()
 
-    turn = (-shift) & mask
+    for there, copy in (
+        (above_after[0], corner_up), (below_after[0], corner_down),
+        (above[0], up_copies[0]), (below[0], down_copies[0]),
+    ):
+        @pl.when(there)
+        def _(copy=copy):
+            copy.start()
+
     turned = [pltpu.roll(w, turn, 1) for w in whole]
     came_from = lane_a + shift
     for b in range(blocks):
@@ -238,10 +275,8 @@
         0,
     )
     block0 = jnp.where(lane_a < -shift, from_left, moved_buf[:, :LANES])
-    block0 = jnp.where(lane_a < new_count, block0, 0.0)
 
     def send(sweep, c, mu):
-        lane32 = lanes(ROWS)
         ghost_out[sweep] = jnp.where(lane32 < HALF, c, pltpu.roll(mu, HALF, 1))
 
         @pl.when(above[0])
@@ -252,7 +287,6 @@
         def _():
             down_copies[sweep].start()
 
-    send(0, block0[:ROWS], block0[ROWS : 2 * ROWS])
     moved_buf[:, :LANES] = block0
 
     @pl.when(after[0])
@@ -294,7 +328,6 @@
     weight_prev = 1.0 / spread_ratio
     update = [None] * blocks
     first_table, second_table = first_buf[...], second_buf[...]
-    lane32 = lanes(ROWS)
     for sweep in range(SWEEPS):
         last = sweep == SWEEPS - 1
         product = jnp.dot(
@@ -325,6 +358,17 @@
             down_copies[sweep].wait_recv()
 
         got_below, got_above = ghost_in[sweep, 0], ghost_in[sweep, 1]
+        if sweep == 0:
+            @pl.when(below_left[0])
+            def _():
+                corner_up.wait_recv()
+
+            @pl.when(above_left[0])
+            def _():
+                corner_down.wait_recv()
+
+            got_below = got_below + corner_in[0]
+            got_above = got_above + corner_in[1]
         ghost = jnp.concatenate(
             [
                 jnp.where(lane32 < HALF, got_below, pltpu.roll(got_above, HALF, 1)),
@@ -371,6 +415,14 @@
     def _():
         tail_copy.wait_send()
 
+    @pl.when(above_after[0])
+    def _():
+        corner_up.wait_send()
+
+    @pl.when(below_after[0])
+    def _():
+        corner_down.wait_send()
+
     for sweep in range(SWEEPS):
         @pl.when(above[0])
         def _():
@@ -415,13 +467,16 @@
             pltpu.VMEM((packed_rows, LANES), F32),
             pltpu.VMEM((SWEEPS, ROWS, LANES), F32),
             pltpu.VMEM((SWEEPS, 2, ROWS, LANES), F32),
+            pltpu.VMEM((ROWS, LANES), F32),
+            pltpu.VMEM((2, ROWS, LANES), F32),
             pltpu.VMEM((5 * ROWS, capacity), F32),
-            pltpu.VMEM((8, LANES), F32),
             pltpu.SemaphoreType.DMA((8,)),
             pltpu.SemaphoreType.DMA((2,)),
             pltpu.SemaphoreType.DMA((2,)),
             pltpu.SemaphoreType.DMA((SWEEPS, 2)),
             pltpu.SemaphoreType.DMA((SWEEPS, 2)),
+            pltpu.SemaphoreType.DMA((2,)),
+            pltpu.SemaphoreType.DMA((2,)),
         ],
         compiler_params=pltpu.CompilerParams(
             collective_id=0, has_side_effects=True, vmem_limit_bytes=60 * 1024 * 1024

time: 16.8 us -> 17.1 us (1.018)
  Pallas kernels: 16 us -> 16.3 us
    pallas_call x1, Pallas kernels: 16 us -> 16.3 us  [local(): pl.pallas_call(functools.partial(kernel, n_seg, n_sub), out_shape=pltpu.V...]
where the time goes in v3:
time: 17.1 us; the launch traced here: 17 us
  Pallas kernels  16.3 us (95%)
  local copies, waits for them, and re-layouts  0.65 us (4%)
    pallas_call x1, Pallas kernels, local(): pl.pallas_call(functools.partial(kernel, n_seg, n_sub), out_shape=pltpu.V...  16.3 us
    unnamed x1, local copies, waits for them, and re-layouts  0.65 us

profile of v3, /device:TPU:0, one launch (start us, length us, event | category | flops | bytes accessed | tf_op | source)
XLA Modules:
  0.0 17.0 jit_solution(2101613802814354403)
XLA Ops:
  0.0 16.3 %smooth.1 = f32[216,128]{1,0:T(8,128)S(1)} custom-call(s32[1,5]{1,0:T(1,128)} %old_cuts.1, s32[1,5]{1,0:T(1,128)} %new_cuts.1, f32[216,128]{1,0:T(8,128)} %bitcast.21, f32[216,128]{1,0:T(8,128)} %bitcast.22, f32[27,512]{1,0:T(8,128)} %prev.1, s32[1,512]{1,0:T(1,128)} %bitcast.23, s32[6,512]{1,0:T(8,128)} %links.1, bf16[176,128]{1,0:T(8,128)(2,1)} %constant.6.clone.first, ...), custom_call_target="tpu_custom_call" | custom-call | tf_op jit(solution)/shard_map/smooth/pallas_call | solution.py:448
  16.3 0.6 %copy.15 = f32[2,27,512]{2,0,1:T(2,128)} copy(f32[2,27,512]{2,0,1:T(2,128)S(1)} %bitcast.20) | data formatting | bytes 221184

commit v4 on v3

--- a/solution.py
+++ b/solution.py
@@ -73,7 +73,8 @@
 def kernel(
     n_seg, n_sub, old_cuts, new_cuts, start, right, prev, refined, links, first, second, inverse,
     out, state_buf, side_buf, prior_buf, flags, link_buf, first_buf, second_buf, inverse_buf,
-    index_buf, block_buf, head_out, tail_out, head_in, tail_in, ghost_out, ghost_in,
+    index_buf, block_buf, head_out0, tail_out0, head_in0, tail_in0,
+    head_out1, tail_out1, head_in1, tail_in1, ghost_out, ghost_in,
     corner_out, corner_in, moved_buf, load_sem, head_sem, tail_sem, ghost_send, ghost_recv,
     corner_send, corner_recv,
 ):
@@ -99,8 +100,8 @@
     for load in loads:
         load.start()
 
-    head_in[...] = jnp.zeros_like(head_in)
-    tail_in[...] = jnp.zeros_like(tail_in)
+    for arriving in (head_in0, tail_in0, head_in1, tail_in1):
+        arriving[...] = jnp.zeros_like(arriving)
     ghost_in[...] = jnp.zeros_like(ghost_in)
     corner_in[...] = jnp.zeros_like(corner_in)
 
@@ -119,12 +120,18 @@
         def _(place=place):
             pl.semaphore_signal(barrier, inc=1, device_id=place, device_id_type=MESH)
 
-    head_copy = pltpu.make_async_remote_copy(
-        src_ref=head_out, dst_ref=head_in, send_sem=head_sem.at[0], recv_sem=head_sem.at[1],
-        device_id=left[1], device_id_type=MESH)
-    tail_copy = pltpu.make_async_remote_copy(
-        src_ref=tail_out, dst_ref=tail_in, send_sem=tail_sem.at[0], recv_sem=tail_sem.at[1],
-        device_id=after[1], device_id_type=MESH)
+    head_copies = [
+        pltpu.make_async_remote_copy(
+            src_ref=source, dst_ref=target, send_sem=head_sem.at[i, 0], recv_sem=head_sem.at[i, 1],
+            device_id=left[1], device_id_type=MESH)
+        for i, (source, target) in enumerate([(head_out0, head_in0), (head_out1, head_in1)])
+    ]
+    tail_copies = [
+        pltpu.make_async_remote_copy(
+            src_ref=source, dst_ref=target, send_sem=tail_sem.at[i, 0], recv_sem=tail_sem.at[i, 1],
+            device_id=after[1], device_id_type=MESH)
+        for i, (source, target) in enumerate([(tail_out0, tail_in0), (tail_out1, tail_in1)])
+    ]
     up_copies, down_copies = [], []
     for sweep in range(SWEEPS):
         up_copies.append(pltpu.make_async_remote_copy(
@@ -158,43 +165,91 @@
     def lanes(rows):
         return lax.broadcasted_iota(jnp.int32, (rows, LANES), 1)
 
-    for i in range(4):
-        loads[i].wait()
-
     pad = jnp.zeros((ROWS - 27, LANES), F32)
     row32 = lax.broadcasted_iota(jnp.int32, (ROWS, LANES), 0)
 
-    def packed(b):
-        cols = pl.ds(b * LANES, LANES)
-        parts = [
-            jnp.concatenate([rows, pad], 0)
-            for rows in (
-                state_buf[pl.ds(2 * b, 27, stride=2 * blocks), :],
-                state_buf[pl.ds(2 * b + 1, 27, stride=2 * blocks), :],
-                side_buf[pl.ds(2 * b, 27, stride=2 * blocks), :],
-                side_buf[pl.ds(2 * b + 1, 27, stride=2 * blocks), :],
-                prior_buf[:, cols],
-            )
-        ]
-        flag = flags[:, cols].astype(F32)
-        parts[4] = jnp.where(row32 == 27, jnp.broadcast_to(flag, (ROWS, LANES)), parts[4])
-        return jnp.concatenate(parts, 0)
-
-    all_rows = 5 * ROWS
-    upper = all_rows // 2
-    whole = [packed(b) for b in range(blocks)]
-    lane_u = lanes(upper)
-    head_out[...] = jnp.where(lane_u < HALF, whole[0][:upper], pltpu.roll(whole[0][upper:], HALF, 1))
-    tail = whole[0]
-    lane_a = lanes(all_rows)
-    window = (lane_u >= old_count - HALF) & (lane_u < old_count)
-    for b in range(1, blocks):
-        slot = lane_a + b * LANES
-        inside = (slot >= old_count - HALF) & (slot < old_count)
-        tail = jnp.where(inside, whole[b], tail)
-        slot_u = lane_u + b * LANES
-        window = window | ((slot_u >= old_count - HALF) & (slot_u < old_count))
-    tail_out[...] = jnp.where(window, tail[:upper], pltpu.roll(tail[upper:], HALF, 1))
+    def component(buffer, b, part):
+        rows = buffer[pl.ds(2 * b + part, 27, stride=2 * blocks), :]
+        return jnp.concatenate([rows, pad], 0)
+
+    def pack_edges(whole, head_out, tail_out):
+        count = whole[0].shape[0]
+        upper = count // 2
+        lane_u, lane_a = lanes(upper), lanes(count)
+        head_out[...] = jnp.where(
+            lane_u < HALF, whole[0][:upper], pltpu.roll(whole[0][upper:], HALF, 1)
+        )
+        tail = whole[0]
+        window = (lane_u >= old_count - HALF) & (lane_u < old_count)
+        for b in range(1, blocks):
+            slot = lane_a + b * LANES
+            inside = (slot >= old_count - HALF) & (slot < old_count)
+            tail = jnp.where(inside, whole[b], tail)
+            slot_u = lane_u + b * LANES
+            window = window | ((slot_u >= old_count - HALF) & (slot_u < old_count))
+        tail_out[...] = jnp.where(window, tail[:upper], pltpu.roll(tail[upper:], HALF, 1))
+        return tail
+
+    def start_edges(i):
+        @pl.when(after[0])
+        def _():
+            tail_copies[i].start()
+
+        @pl.when(left[0])
+        def _():
+            head_copies[i].start()
+
+    def rotate(whole, first_row):
+        turned = [pltpu.roll(w, turn, 1) for w in whole]
+        came_from = lanes(whole[0].shape[0]) + shift
+        for b in range(blocks):
+            mine = turned[b]
+            if b > 0:
+                mine = jnp.where(came_from < 0, turned[b - 1], mine)
+            if b < blocks - 1:
+                mine = jnp.where(came_from >= LANES, turned[b + 1], mine)
+            rows = slice(first_row, first_row + whole[0].shape[0])
+            moved_buf[rows, b * LANES : (b + 1) * LANES] = mine
+
+    def from_edge(arrived, amount):
+        return jnp.concatenate(
+            [
+                pltpu.roll(arrived[...], amount & mask, 1),
+                pltpu.roll(arrived[...], (amount + HALF) & mask, 1),
+            ],
+            0,
+        )
+
+    edge = old_end - new_first
+
+    def arrive(i, first_row, count, head_in, tail_in):
+        @pl.when(left[0])
+        def _():
+            tail_copies[i].wait_recv()
+
+        @pl.when(after[0])
+        def _():
+            head_copies[i].wait_recv()
+
+        from_left = from_edge(tail_in, left_first - new_first)
+        from_right = from_edge(head_in, edge)
+        lane_a = lanes(count)
+        result = []
+        for b in range(blocks):
+            slot = lane_a + b * LANES
+            part = moved_buf[first_row : first_row + count, b * LANES : (b + 1) * LANES]
+            if b == 0:
+                part = jnp.where(slot < -shift, from_left, part)
+            part = jnp.where(slot >= edge, from_right, part)
+            result.append(jnp.where(slot < new_count, part, 0.0))
+        return result
+
+    loads[0].wait()
+    whole = [
+        jnp.concatenate([component(state_buf, b, 0), component(state_buf, b, 1)], 0)
+        for b in range(blocks)
+    ]
+    tail = pack_edges(whole, head_out0, tail_out0)
 
     turn = (-shift) & mask
     lane32 = lanes(ROWS)
@@ -219,13 +274,7 @@
     has_after = jnp.minimum(n_sub - 1 - sub, 1)
     pl.semaphore_wait(barrier, jnp.minimum(sub, 1) + has_after + seg_sides * (1 + has_after))
 
-    @pl.when(after[0])
-    def _():
-        tail_copy.start()
-
-    @pl.when(left[0])
-    def _():
-        head_copy.start()
+    start_edges(0)
 
     for there, copy in (
         (above_after[0], corner_up), (below_after[0], corner_down),
@@ -235,15 +284,20 @@
         def _(copy=copy):
             copy.start()
 
-    turned = [pltpu.roll(w, turn, 1) for w in whole]
-    came_from = lane_a + shift
+    for i in range(1, 4):
+        loads[i].wait()
+    others = []
     for b in range(blocks):
-        mine = turned[b]
-        if b > 0:
-            mine = jnp.where(came_from < 0, turned[b - 1], mine)
-        if b < blocks - 1:
-            mine = jnp.where(came_from >= LANES, turned[b + 1], mine)
-        moved_buf[:, b * LANES : (b + 1) * LANES] = mine
+        cols = pl.ds(b * LANES, LANES)
+        flag = flags[:, cols].astype(F32)
+        prior = jnp.concatenate([prior_buf[:, cols], pad], 0)
+        prior = jnp.where(row32 == 27, jnp.broadcast_to(flag, (ROWS, LANES)), prior)
+        others.append(
+            jnp.concatenate([component(side_buf, b, 0), component(side_buf, b, 1), prior], 0)
+        )
+    pack_edges(others, head_out1, tail_out1)
+    start_edges(1)
+    rotate(whole, 0)
 
     loads[4].wait()
     for b in range(blocks):
@@ -262,20 +316,6 @@
     for i in range(5, 8):
         loads[i].wait()
 
-    @pl.when(left[0])
-    def _():
-        tail_copy.wait_recv()
-
-    offset = left_first - new_first
-    from_left = jnp.concatenate(
-        [
-            pltpu.roll(tail_in[...], offset & mask, 1),
-            pltpu.roll(tail_in[...], (offset + HALF) & mask, 1),
-        ],
-        0,
-    )
-    block0 = jnp.where(lane_a < -shift, from_left, moved_buf[:, :LANES])
-
     def send(sweep, c, mu):
         ghost_out[sweep] = jnp.where(lane32 < HALF, c, pltpu.roll(mu, HALF, 1))
 
@@ -287,41 +327,27 @@
         def _():
             down_copies[sweep].start()
 
-    moved_buf[:, :LANES] = block0
-
-    @pl.when(after[0])
-    def _():
-        head_copy.wait_recv()
-
-    edge = old_end - new_first
-    from_right = jnp.concatenate(
-        [
-            pltpu.roll(head_in[...], edge & mask, 1),
-            pltpu.roll(head_in[...], (edge + HALF) & mask, 1),
-        ],
-        0,
-    )
-    state, coefficients = [], []
-    inverse_mass = inverse_buf[...]
-    for b in range(blocks):
-        slot = lane_a + b * LANES
-        whole_b = moved_buf[:, b * LANES : (b + 1) * LANES]
-        whole_b = jnp.where(slot >= edge, from_right, whole_b)
-        whole_b = jnp.where(slot < new_count, whole_b, 0.0)
-        state.append(whole_b[: 2 * ROWS])
-        prior = whole_b[4 * ROWS :]
-        flag = jnp.broadcast_to(prior[27:28], (ROWS, LANES))
-        inverse_lumped = inverse_mass * (1.0 + 7.0 * flag)
-        stiff = (1.0 - 0.5 * flag) * inverse_lumped * (1.0 / 6.0)
-        coefficients.append(
-            (
-                whole_b[2 * ROWS : 3 * ROWS] * inverse_lumped,
-                whole_b[3 * ROWS : 4 * ROWS] * inverse_lumped,
-                time_step * stiff * (1.0 - prior * prior),
-                gradient_energy * stiff,
-                3.0 * prior * prior - 1.0,
+    state = arrive(0, 0, 2 * ROWS, head_in0, tail_in0)
+    rotate(others, 2 * ROWS)
+
+    def coefficients_of():
+        result = []
+        inverse_mass = inverse_buf[...]
+        for part in arrive(1, 2 * ROWS, 3 * ROWS, head_in1, tail_in1):
+            prior = part[2 * ROWS :]
+            flag = jnp.broadcast_to(prior[27:28], (ROWS, LANES))
+            inverse_lumped = inverse_mass * (1.0 + 7.0 * flag)
+            stiff = (1.0 - 0.5 * flag) * inverse_lumped * (1.0 / 6.0)
+            result.append(
+                (
+                    part[:ROWS] * inverse_lumped,
+                    part[ROWS : 2 * ROWS] * inverse_lumped,
+                    time_step * stiff * (1.0 - prior * prior),
+                    gradient_energy * stiff,
+                    3.0 * prior * prior - 1.0,
+                )
             )
-        )
+        return result
 
     spread_ratio = 2.0
     half_width = 0.5
@@ -348,6 +374,8 @@
             for number in range(blocks):
                 total = pick(total, sources[number], number, b)
             faces.append(total)
+        if sweep == 0:
+            coefficients = coefficients_of()
 
         @pl.when(below[0])
         def _():
@@ -409,11 +437,13 @@
 
     @pl.when(left[0])
     def _():
-        head_copy.wait_send()
+        for copy in head_copies:
+            copy.wait_send()
 
     @pl.when(after[0])
     def _():
-        tail_copy.wait_send()
+        for copy in tail_copies:
+            copy.wait_send()
 
     @pl.when(above_after[0])
     def _():
@@ -438,7 +468,6 @@
     first, second, inverse = element_tables()
     any_space = pl.BlockSpec(memory_space=pl.ANY)
     smem = pl.BlockSpec(memory_space=pltpu.SMEM)
-    packed_rows = 5 * ROWS // 2
     blocks = capacity // LANES
 
     def by_node(array):
@@ -461,18 +490,16 @@
             pltpu.VMEM(inverse.shape, F32),
             pltpu.VMEM((FACE_ROWS, capacity), jnp.int32),
             pltpu.VMEM((FACE_ROWS, capacity), jnp.int32),
-            pltpu.VMEM((packed_rows, LANES), F32),
-            pltpu.VMEM((packed_rows, LANES), F32),
-            pltpu.VMEM((packed_rows, LANES), F32),
-            pltpu.VMEM((packed_rows, LANES), F32),
+            *[pltpu.VMEM((ROWS, LANES), F32)] * 4,
+            *[pltpu.VMEM((3 * ROWS // 2, LANES), F32)] * 4,
             pltpu.VMEM((SWEEPS, ROWS, LANES), F32),
             pltpu.VMEM((SWEEPS, 2, ROWS, LANES), F32),
             pltpu.VMEM((ROWS, LANES), F32),
             pltpu.VMEM((2, ROWS, LANES), F32),
             pltpu.VMEM((5 * ROWS, capacity), F32),
             pltpu.SemaphoreType.DMA((8,)),
-            pltpu.SemaphoreType.DMA((2,)),
-            pltpu.SemaphoreType.DMA((2,)),
+            pltpu.SemaphoreType.DMA((2, 2)),
+            pltpu.SemaphoreType.DMA((2, 2)),
             pltpu.SemaphoreType.DMA((SWEEPS, 2)),
             pltpu.SemaphoreType.DMA((SWEEPS, 2)),
             pltpu.SemaphoreType.DMA((2,)),

time: 17.1 us -> 17.2 us (level)
  no operation moved by 1% of the time
where the time goes in v4:
time: 17.2 us; the launch traced here: 17 us
  Pallas kernels  16.3 us (95%)
  local copies, waits for them, and re-layouts  0.65 us (4%)
    pallas_call x1, Pallas kernels, local(): pl.pallas_call(functools.partial(kernel, n_seg, n_sub), out_shape=pltpu.V...  16.3 us
    unnamed x1, local copies, waits for them, and re-layouts  0.65 us

profile of v4, /device:TPU:0, one launch (start us, length us, event | category | flops | bytes accessed | tf_op | source)
XLA Modules:
  0.0 17.0 jit_solution(9403958402529402318)
XLA Ops:
  0.0 16.3 %smooth.1 = f32[216,128]{1,0:T(8,128)S(1)} custom-call(s32[1,5]{1,0:T(1,128)} %old_cuts.1, s32[1,5]{1,0:T(1,128)} %new_cuts.1, f32[216,128]{1,0:T(8,128)} %bitcast.21, f32[216,128]{1,0:T(8,128)} %bitcast.22, f32[27,512]{1,0:T(8,128)} %prev.1, s32[1,512]{1,0:T(1,128)} %bitcast.23, s32[6,512]{1,0:T(8,128)} %links.1, bf16[176,128]{1,0:T(8,128)(2,1)} %constant.6.clone.first, ...), custom_call_target="tpu_custom_call" | custom-call | tf_op jit(solution)/shard_map/smooth/pallas_call | solution.py:477
  16.4 0.6 %copy.15 = f32[2,27,512]{2,0,1:T(2,128)} copy(f32[2,27,512]{2,0,1:T(2,128)S(1)} %bitcast.20) | data formatting | bytes 221184

commit v5 on v4

--- a/solution.py
+++ b/solution.py
@@ -249,8 +249,6 @@
         jnp.concatenate([component(state_buf, b, 0), component(state_buf, b, 1)], 0)
         for b in range(blocks)
     ]
-    tail = pack_edges(whole, head_out0, tail_out0)
-
     turn = (-shift) & mask
     lane32 = lanes(ROWS)
     slot32 = lane32 & (HALF - 1)
@@ -265,20 +263,26 @@
     ghost_out[0] = jnp.where(
         (slot32 >= -shift) & (slot32 < new_count), both(whole[0], turn), 0.0
     )
+    seg_sides = jnp.minimum(seg, 1) + jnp.minimum(n_seg - 1 - seg, 1)
+    has_after = jnp.minimum(n_sub - 1 - sub, 1)
+    pl.semaphore_wait(barrier, jnp.minimum(sub, 1) + has_after + seg_sides * (1 + has_after))
+
+    for there, copy in ((above[0], up_copies[0]), (below[0], down_copies[0])
+    ):
+        @pl.when(there)
+        def _(copy=copy):
+            copy.start()
+
+    tail = pack_edges(whole, head_out0, tail_out0)
+
+    start_edges(0)
+
     next_count = new_cuts[0, jnp.minimum(sub + 2, n_sub)] - new_end
     corner_out[...] = jnp.where(
         (slot32 < old_end - new_end) & (slot32 < next_count), both(tail, old_first - new_end), 0.0
     )
 
-    seg_sides = jnp.minimum(seg, 1) + jnp.minimum(n_seg - 1 - seg, 1)
-    has_after = jnp.minimum(n_sub - 1 - sub, 1)
-    pl.semaphore_wait(barrier, jnp.minimum(sub, 1) + has_after + seg_sides * (1 + has_after))
-
-    start_edges(0)
-
-    for there, copy in (
-        (above_after[0], corner_up), (below_after[0], corner_down),
-        (above[0], up_copies[0]), (below[0], down_copies[0]),
+    for there, copy in ((above_after[0], corner_up), (below_after[0], corner_down)
     ):
         @pl.when(there)
         def _(copy=copy):

time: 17.2 us -> 16.8 us (0.977)
  Pallas kernels: 16.3 us -> 16 us
    pallas_call x1, Pallas kernels: 16.3 us -> 16 us  [local(): pl.pallas_call(functools.partial(kernel, n_seg, n_sub), out_shape=pltpu.V...]
where the time goes in v5:
time: 16.8 us; the launch traced here: 16.7 us
  Pallas kernels  16 us (95%)
  local copies, waits for them, and re-layouts  0.65 us (4%)
    pallas_call x1, Pallas kernels, local(): pl.pallas_call(functools.partial(kernel, n_seg, n_sub), out_shape=pltpu.V...  16 us
    unnamed x1, local copies, waits for them, and re-layouts  0.65 us

profile of v5, /device:TPU:0, one launch (start us, length us, event | category | flops | bytes accessed | tf_op | source)
XLA Modules:
  0.0 16.7 jit_solution(14878576941268060039)
XLA Ops:
  0.0 16.0 %smooth.1 = f32[216,128]{1,0:T(8,128)S(1)} custom-call(s32[1,5]{1,0:T(1,128)} %old_cuts.1, s32[1,5]{1,0:T(1,128)} %new_cuts.1, f32[216,128]{1,0:T(8,128)} %bitcast.21, f32[216,128]{1,0:T(8,128)} %bitcast.22, f32[27,512]{1,0:T(8,128)} %prev.1, s32[1,512]{1,0:T(1,128)} %bitcast.23, s32[6,512]{1,0:T(8,128)} %links.1, bf16[176,128]{1,0:T(8,128)(2,1)} %constant.6.clone.first, ...), custom_call_target="tpu_custom_call" | custom-call | tf_op jit(solution)/shard_map/smooth/pallas_call | solution.py:481
  16.0 0.6 %copy.15 = f32[2,27,512]{2,0,1:T(2,128)} copy(f32[2,27,512]{2,0,1:T(2,128)S(1)} %bitcast.20) | data formatting | bytes 221184

commit v6 on v5

--- a/solution.py
+++ b/solution.py
@@ -97,8 +97,7 @@
             ]
         )
     ]
-    for load in loads:
-        load.start()
+    loads[0].start()
 
     for arriving in (head_in0, tail_in0, head_in1, tail_in1):
         arriving[...] = jnp.zeros_like(arriving)
@@ -119,6 +118,8 @@
         @pl.when(there)
         def _(place=place):
             pl.semaphore_signal(barrier, inc=1, device_id=place, device_id_type=MESH)
+    for load in loads[1:]:
+        load.start()
 
     head_copies = [
         pltpu.make_async_remote_copy(

time: 16.8 us -> 16.8 us (level)
  no operation moved by 1% of the time
where the time goes in v6:
time: 16.8 us; the launch traced here: 16.6 us
  Pallas kernels  16 us (95%)
  local copies, waits for them, and re-layouts  0.65 us (4%)
    pallas_call x1, Pallas kernels, local(): pl.pallas_call(functools.partial(kernel, n_seg, n_sub), out_shape=pltpu.V...  16 us
    unnamed x1, local copies, waits for them, and re-layouts  0.65 us

profile of v6, /device:TPU:0, one launch (start us, length us, event | category | flops | bytes accessed | tf_op | source)
XLA Modules:
  0.0 16.6 jit_solution(17526963955850121556)
XLA Ops:
  0.0 16.0 %smooth.1 = f32[216,128]{1,0:T(8,128)S(1)} custom-call(s32[1,5]{1,0:T(1,128)} %old_cuts.1, s32[1,5]{1,0:T(1,128)} %new_cuts.1, f32[216,128]{1,0:T(8,128)} %bitcast.21, f32[216,128]{1,0:T(8,128)} %bitcast.22, f32[27,512]{1,0:T(8,128)} %prev.1, s32[1,512]{1,0:T(1,128)} %bitcast.23, s32[6,512]{1,0:T(8,128)} %links.1, bf16[176,128]{1,0:T(8,128)(2,1)} %constant.6.clone.first, ...), custom_call_target="tpu_custom_call" | custom-call | tf_op jit(solution)/shard_map/smooth/pallas_call | solution.py:482
  16.0 0.6 %copy.15 = f32[2,27,512]{2,0,1:T(2,128)} copy(f32[2,27,512]{2,0,1:T(2,128)S(1)} %bitcast.20) | data formatting | bytes 221184

commit v7 on v6

--- a/solution.py
+++ b/solution.py
@@ -264,46 +264,6 @@
     ghost_out[0] = jnp.where(
         (slot32 >= -shift) & (slot32 < new_count), both(whole[0], turn), 0.0
     )
-    seg_sides = jnp.minimum(seg, 1) + jnp.minimum(n_seg - 1 - seg, 1)
-    has_after = jnp.minimum(n_sub - 1 - sub, 1)
-    pl.semaphore_wait(barrier, jnp.minimum(sub, 1) + has_after + seg_sides * (1 + has_after))
-
-    for there, copy in ((above[0], up_copies[0]), (below[0], down_copies[0])
-    ):
-        @pl.when(there)
-        def _(copy=copy):
-            copy.start()
-
-    tail = pack_edges(whole, head_out0, tail_out0)
-
-    start_edges(0)
-
-    next_count = new_cuts[0, jnp.minimum(sub + 2, n_sub)] - new_end
-    corner_out[...] = jnp.where(
-        (slot32 < old_end - new_end) & (slot32 < next_count), both(tail, old_first - new_end), 0.0
-    )
-
-    for there, copy in ((above_after[0], corner_up), (below_after[0], corner_down)
-    ):
-        @pl.when(there)
-        def _(copy=copy):
-            copy.start()
-
-    for i in range(1, 4):
-        loads[i].wait()
-    others = []
-    for b in range(blocks):
-        cols = pl.ds(b * LANES, LANES)
-        flag = flags[:, cols].astype(F32)
-        prior = jnp.concatenate([prior_buf[:, cols], pad], 0)
-        prior = jnp.where(row32 == 27, jnp.broadcast_to(flag, (ROWS, LANES)), prior)
-        others.append(
-            jnp.concatenate([component(side_buf, b, 0), component(side_buf, b, 1), prior], 0)
-        )
-    pack_edges(others, head_out1, tail_out1)
-    start_edges(1)
-    rotate(whole, 0)
-
     loads[4].wait()
     for b in range(blocks):
         cols = pl.ds(b * LANES, LANES)
@@ -318,6 +278,46 @@
         link = jnp.concatenate(parts, 0)
         index_buf[:, cols] = link & mask
         block_buf[:, cols] = link >> 7
+    seg_sides = jnp.minimum(seg, 1) + jnp.minimum(n_seg - 1 - seg, 1)
+    has_after = jnp.minimum(n_sub - 1 - sub, 1)
+    pl.semaphore_wait(barrier, jnp.minimum(sub, 1) + has_after + seg_sides * (1 + has_after))
+
+    for there, copy in ((above[0], up_copies[0]), (below[0], down_copies[0])
+    ):
+        @pl.when(there)
+        def _(copy=copy):
+            copy.start()
+
+    tail = pack_edges(whole, head_out0, tail_out0)
+
+    start_edges(0)
+
+    next_count = new_cuts[0, jnp.minimum(sub + 2, n_sub)] - new_end
+    corner_out[...] = jnp.where(
+        (slot32 < old_end - new_end) & (slot32 < next_count), both(tail, old_first - new_end), 0.0
+    )
+
+    for there, copy in ((above_after[0], corner_up), (below_after[0], corner_down)
+    ):
+        @pl.when(there)
+        def _(copy=copy):
+            copy.start()
+
+    for i in range(1, 4):
+        loads[i].wait()
+    others = []
+    for b in range(blocks):
+        cols = pl.ds(b * LANES, LANES)
+        flag = flags[:, cols].astype(F32)
+        prior = jnp.concatenate([prior_buf[:, cols], pad], 0)
+        prior = jnp.where(row32 == 27, jnp.broadcast_to(flag, (ROWS, LANES)), prior)
+        others.append(
+            jnp.concatenate([component(side_buf, b, 0), component(side_buf, b, 1), prior], 0)
+        )
+    pack_edges(others, head_out1, tail_out1)
+    start_edges(1)
+    rotate(whole, 0)
+
     for i in range(5, 8):
         loads[i].wait()
 

time: 16.8 us -> 16.8 us (level)
  no operation moved by 1% of the time
where the time goes in v7:
time: 16.8 us; the launch traced here: 16.6 us
  Pallas kernels  16 us (95%)
  local copies, waits for them, and re-layouts  0.65 us (4%)
    pallas_call x1, Pallas kernels, local(): pl.pallas_call(functools.partial(kernel, n_seg, n_sub), out_shape=pltpu.V...  16 us
    unnamed x1, local copies, waits for them, and re-layouts  0.65 us

profile of v7, /device:TPU:0, one launch (start us, length us, event | category | flops | bytes accessed | tf_op | source)
XLA Modules:
  0.0 16.6 jit_solution(14612230652872450527)
XLA Ops:
  0.0 16.0 %smooth.1 = f32[216,128]{1,0:T(8,128)S(1)} custom-call(s32[1,5]{1,0:T(1,128)} %old_cuts.1, s32[1,5]{1,0:T(1,128)} %new_cuts.1, f32[216,128]{1,0:T(8,128)} %bitcast.21, f32[216,128]{1,0:T(8,128)} %bitcast.22, f32[27,512]{1,0:T(8,128)} %prev.1, s32[1,512]{1,0:T(1,128)} %bitcast.23, s32[6,512]{1,0:T(8,128)} %links.1, bf16[176,128]{1,0:T(8,128)(2,1)} %constant.6.clone.first, ...), custom_call_target="tpu_custom_call" | custom-call | tf_op jit(solution)/shard_map/smooth/pallas_call | solution.py:482
  16.0 0.6 %copy.15 = f32[2,27,512]{2,0,1:T(2,128)} copy(f32[2,27,512]{2,0,1:T(2,128)S(1)} %bitcast.20) | data formatting | bytes 221184
